TPU v7x, 32 devices: a whole 2x2x4 slice. The times are simulated.
32 devices in a mesh: tm: 16 (over z, y, x), sens: 2 (over core).
Axes of the slice: x: 2, y: 2, z: 4, core: 2. Of those that a mesh axis runs over, the one named last changes fastest.
Arguments:
- telemetry: float32 [8192, 512], P('tm', 'sens'), may hold values from -6 to 6
- present: int32 [512, 8], P('tm', 'sens'), may hold values 0 or 1
- transition: float32 [128, 128], replicated, may hold values from -1 to 1, as said below
- sensing: float32 [512, 128], P('sens'), may hold values from -3 to 3, as said below
- filter_gain: float32 [128, 512], P(None, 'sens'), may hold values from -1 to 1, as said below
- smooth_gain: float32 [128, 128], replicated, may hold values from -1 to 1, as said below
- initial_state: float32 [128], replicated, may hold values from -6 to 6
Outputs:
- new_transition: float32 [128, 128], replicated
- new_sensing: float32 [512, 128], P('sens')
- smoothed: float32 [8192, 128], P('tm')
Inputs may be any that keep to these rules, and one draw needn't show every extreme that they name: `transition`: the previous iteration's estimate of the transition matrix; every entry lies between -1 and 1. `sensing`: the previous iteration's estimate of the observation matrix; every entry lies between -3 and 3. `filter_gain`: the previous iteration's steady filter gain; every entry lies between -1 and 1. `smooth_gain`: the previous iteration's steady smoother gain; every entry lies between -1 and 1.
All inputs are finite; a program needn't handle non-finite values. No bound on the sum of `present` on one device may be relied on, other than what follows from the above.
Results may differ from a plain program's by a relative error of at most 0.014.
Values sent between devices are 32-bit elements; how exact they have to be, the bound alone decides.
A program may use at most 128 MiB of HBM per device.

v0:
```python
import functools

import jax
import jax.numpy as jnp
from jax import lax
from jax.experimental import pallas as pl
from jax.experimental.pallas import tpu as pltpu
from jax.sharding import PartitionSpec as P

RIDGE = 0.001
GROUP = 4
PIVOT = 32
TOGETHER = 4
REDUCERS = 16
MESH = pl.DeviceIdType.MESH
VMEM = pltpu.VMEM
F32 = jnp.float32
LIMIT = 48 * 1024 * 1024


def mm(a, b):
    return jnp.dot(a, b, precision=lax.Precision.HIGHEST, preferred_element_type=F32)


def mv(a, b):
    return jnp.dot(a, b, precision=lax.Precision.HIGH, preferred_element_type=F32)


def mm_tn(a, b):
    return lax.dot_general(
        a, b, (((0,), (0,)), ((), ())),
        precision=lax.Precision.HIGHEST, preferred_element_type=F32,
    )


def mm_nt(a, b):
    return lax.dot_general(
        a, b, (((1,), (1,)), ((), ())),
        precision=lax.Precision.HIGHEST, preferred_element_type=F32,
    )


def row_ids(shape):
    return lax.broadcasted_iota(jnp.int32, shape, 0)


def shift_down(v, by):
    if by % 8 == 0:
        return jnp.concatenate([jnp.zeros((by, v.shape[1]), F32), v[:-by]], axis=0)
    return jnp.where(row_ids(v.shape) >= by, pltpu.roll(v, by, 0), 0.0)


def shift_up(v, by):
    rows = v.shape[0]
    if by % 8 == 0:
        return jnp.concatenate([v[by:], jnp.zeros((by, v.shape[1]), F32)], axis=0)
    return jnp.where(row_ids(v.shape) < rows - by, pltpu.roll(v, rows - by, 0), 0.0)


def vmem_call(body, out_shape, scratch=(), in_specs=None, remote=None):
    params = dict(vmem_limit_bytes=LIMIT)
    if remote is not None:
        params.update(collective_id=remote, has_side_effects=True)
    return pl.pallas_call(
        body,
        out_shape=out_shape,
        in_specs=in_specs,
        out_specs=jax.tree.map(lambda _: pl.BlockSpec(memory_space=VMEM), out_shape),
        scratch_shapes=list(scratch),
        compiler_params=pltpu.CompilerParams(**params),
    )


def in_vmem(count):
    return [pl.BlockSpec(memory_space=VMEM)] * count


def shaped(*shape):
    return jax.ShapeDtypeStruct(shape, F32)


def push_kernel(tele, flags, trans, sense, gain, masked, push, corr):
    rows, sensors = tele.shape
    segs, blocks = flags.shape
    seg_len, width = rows // segs, sensors // blocks
    spread = jnp.where(
        lax.broadcasted_iota(jnp.int32, (blocks, sensors), 1) // width
        == lax.broadcasted_iota(jnp.int32, (blocks, sensors), 0), 1.0, 0.0)
    wide = jnp.dot(flags[...], spread, preferred_element_type=F32)
    step = jnp.broadcast_to(wide[:, None, :], (segs, seg_len, sensors)).reshape(rows, sensors)
    values = tele[...] * step
    masked[...] = values
    push[...] = mm_nt(values, gain[...])
    moved = mm(sense[...], trans[...])
    for g in range(blocks):
        part = slice(g * width, (g + 1) * width)
        corr[g] = lax.dot_general(
            moved[part], gain[:, part], (((0,), (1,)), ((), ())),
            precision=lax.Precision.HIGHEST, preferred_element_type=F32)


def remote(src, dst, send, recv, where):
    return pltpu.make_async_remote_copy(
        src_ref=src, dst_ref=dst, send_sem=send, recv_sem=recv,
        device_id=where, device_id_type=MESH)


def pair_kernel(push, corr, flags, push_in, corr_in, flags_in, send, recv):
    tm, core = lax.axis_index("tm"), lax.axis_index("sens")
    other = (tm, 1 - core)
    barrier = pltpu.get_barrier_semaphore()
    pl.semaphore_signal(barrier, inc=1, device_id=other, device_id_type=MESH)
    pl.semaphore_wait(barrier, 1)
    half = push.shape[0] // 2
    theirs = pl.ds(pl.multiple_of((1 - core) * half, half), half)
    copies = [
        remote(corr, corr_in, send.at[0], recv.at[0], other),
        remote(push.at[theirs], push_in, send.at[1], recv.at[1], other),
        remote(flags, flags_in, send.at[2], recv.at[2], other),
    ]
    for copy in copies:
        copy.start()
    for copy in copies:
        copy.wait()


def maps_kernel(seg_len, push, push_in, corr, corr_in, flags, flags_in, trans,
                powers, ends, local, chunk, tree):
    core = lax.axis_index("sens")
    segs = ends.shape[0]
    width = trans.shape[0]
    blocks = corr.shape[0]
    levels = seg_len.bit_length() - 1

    def one(k):
        row = core * segs + k
        q = trans[...].T
        for g in range(blocks):
            q = q - flags[row, g] * corr[g] - flags_in[row, g] * corr_in[g]
        mine = pl.ds(pl.multiple_of(row * seg_len, seg_len), seg_len)
        here = pl.ds(pl.multiple_of(k * seg_len, seg_len), seg_len)
        v = push[mine] + push_in[here]
        for s in range(levels):
            powers[s, k] = q
            t = mm(jnp.concatenate([q, v], axis=0), q)
            v = v + shift_down(t[width:], 1 << s)
            q = t[:width]
        local[here] = v
        ends[k] = q
        tree[k, :width] = q
        tree[k, width:] = jnp.broadcast_to(v[seg_len - 1:], (8, width))

    unroll = 4

    def several(i, carry):
        for j in range(unroll):
            one(i * unroll + j)
        return carry

    lax.fori_loop(0, segs // unroll, several, 0)
    span = 1
    while span < segs:
        for k in range(0, segs, 2 * span):
            tree[k] = compose(tree[k], tree[k + span])
        span *= 2
    chunk[...] = tree[0]


def compose(first, second):
    width = second.shape[1]
    t = mm(first, second[:width])
    return jnp.concatenate([t[:width], t[width:] + second[width:]], axis=0)


def follow(x, step):
    width = step.shape[1]
    return mv(x, step[:width]) + step[width:]


def carry_kernel(n, chunk, start, entry, pair, chip, group, arrived, leaving, send, recv):
    tm, core = lax.axis_index("tm"), lax.axis_index("sens")
    place, mine = lax.rem(tm, GROUP), lax.div(tm, GROUP)
    groups = n // GROUP
    other = (tm, 1 - core)
    base = tm - place
    peers = [(base + lax.rem(place + k, GROUP), core) for k in range(1, GROUP)]
    barrier = pltpu.get_barrier_semaphore()
    chain = [(lax.rem(tm + by, n), core) for by in (GROUP, n - GROUP)]
    for peer in [other] + peers + chain:
        pl.semaphore_signal(barrier, inc=1, device_id=peer, device_id_type=MESH)
    pl.semaphore_wait(barrier, GROUP + 2)

    swap = remote(chunk, pair, send.at[0], recv.at[0], other)
    swap.start()
    swap.wait()
    own, their = chunk[...], pair[...]
    first = jnp.where(core == 0, own, their)
    chip[...] = compose(first, jnp.where(core == 0, their, own))
    copies = []
    for k, peer in enumerate(peers):
        copy = remote(chip, group.at[k], send.at[1 + k], recv.at[1 + k], peer)
        copy.start()
        copies.append(copy)
    for copy in copies:
        copy.wait()
    held = [chip[...]] + [group[k] for k in range(GROUP - 1)]
    ordered = []
    for p in range(GROUP):
        value = held[0]
        for k in range(1, GROUP):
            value = jnp.where(lax.rem(place - k + GROUP, GROUP) == p, held[k], value)
        ordered.append(value)
    low, high = compose(ordered[0], ordered[1]), compose(ordered[2], ordered[3])
    whole = compose(low, high)
    hand = remote(leaving, arrived, send.at[GROUP], recv.at[GROUP], (tm + GROUP, core))

    @pl.when(mine == 0)
    def _():
        arrived[...] = start[...]

    @pl.when(mine > 0)
    def _():
        remote(leaving, arrived, send.at[GROUP], recv.at[GROUP], (tm - GROUP, core)).wait_recv()

    x = arrived[...]
    leaving[...] = follow(x, whole)

    @pl.when(mine < groups - 1)
    def _():
        hand.start()

    x = jnp.where(place >= 2, follow(x, low), x)
    before = jnp.where(place >= 2, ordered[2], ordered[0])
    x = jnp.where(lax.rem(place, 2) == 1, follow(x, before), x)
    entry[...] = jnp.where(core == 1, follow(x, first), x)

    @pl.when(mine < groups - 1)
    def _():
        hand.wait_send()


def filter_kernel(n, seg_len, entry, powers, ends, local, trans, smooth,
                  drive_scan, gains, shift, final, states, filtered):
    levels, segs = powers.shape[:2]
    width = trans.shape[0]
    rows = segs * seg_len

    x = entry[...]
    for k in range(segs):
        states[k] = x
        x = mv(x, ends[k]) + local[(k + 1) * seg_len - 1:(k + 1) * seg_len]

    def one(k):
        here = pl.ds(pl.multiple_of(k * seg_len, seg_len), seg_len)
        w = jnp.concatenate([states[k]] * (seg_len // 8), axis=0)
        ids = row_ids(w.shape)
        for s in range(levels):
            w = jnp.where((ids // (1 << s)) % 2 == 1, mv(w, powers[s, k]), w)
        filtered[here] = local[here] + mv(w, powers[0, k])

    unroll = 4

    def several(i, carry):
        for j in range(unroll):
            one(i * unroll + j)
        return carry

    lax.fori_loop(0, segs // unroll, several, 0)
    f = filtered[...]
    ahead = mm_nt(f, trans[...])
    v = f - mm_nt(ahead, smooth[...])
    last = jnp.broadcast_to(ahead[rows - 1:], (8, width))
    final[...] = last
    p = smooth[...].T
    span, level = 1, 0
    while span < rows:
        gains[level] = p
        t = mm(jnp.concatenate([p, v], axis=0), p)
        v = v + shift_up(t[width:], span)
        p = t[:width]
        span, level = span * 2, level + 1
    gains[level] = p
    drive_scan[...] = v
    is_last = (lax.axis_index("tm") == n - 1) & (lax.axis_index("sens") == 1)
    s = jnp.broadcast_to(v[:1], (8, width))
    shift[...] = jnp.where(is_last, s + mm(last, p), s)


def smooth_kernel(n, drive_scan, gains, shift, final, out, entry, shifts, send, recv):
    tm, core = lax.axis_index("tm"), lax.axis_index("sens")
    chunks = 2 * n
    me = tm * 2 + core
    half, width = drive_scan.shape
    barrier = pltpu.get_barrier_semaphore()

    def place(k):
        c = lax.rem(me + k, chunks)
        return (lax.div(c, 2), lax.rem(c, 2))

    def greet(k, carry):
        pl.semaphore_signal(barrier, inc=1, device_id=place(k), device_id_type=MESH)
        return carry

    lax.fori_loop(1, chunks, greet, 0)
    pl.semaphore_wait(barrier, chunks - 1)

    def launch(k, carry):
        remote(shift, shifts.at[me], send.at[k], recv.at[me], place(k)).start()
        return carry

    lax.fori_loop(1, chunks, launch, 0)
    shifts[me] = shift[...]

    def land(k, carry):
        c = lax.rem(me + k, chunks)
        remote(shift, shifts.at[c], send.at[k], recv.at[c], place(k)).wait()
        return carry

    lax.fori_loop(1, chunks, land, 0)
    v = shifts[:, 0, :]
    levels = gains.shape[0] - 1
    p = gains[levels]
    span = 1
    while span < chunks:
        t = mm(jnp.concatenate([p, v], axis=0), p)
        v = v + shift_up(t[width:], span)
        p = t[:width]
        span *= 2
    x = jnp.sum(jnp.where(row_ids(v.shape) == me + 1, v, 0.0), axis=0, keepdims=True)
    x = jnp.where(me == chunks - 1, final[...], jnp.broadcast_to(x, (8, width)))
    after = jnp.where(row_ids(v.shape) == 2 * tm + 2, v, 0.0)
    entry[...] = jnp.broadcast_to(jnp.sum(after, axis=0, keepdims=True), (8, width))
    w = x
    ids = 7 - row_ids(w.shape)
    for s in range(3):
        w = jnp.where((ids // (1 << s)) % 2 == 1, mv(w, gains[s]), w)
    w = mv(w, gains[0])
    for s in range(3, levels):
        w = jnp.concatenate([mv(w, gains[s]), w], axis=0)
    mine = pl.ds(pl.multiple_of(core * half, half), half)
    out[mine] = drive_scan[...] + w
    swap = remote(out.at[mine], out.at[mine], send.at[0], recv.at[chunks], (tm, 1 - core))
    swap.start()
    swap.wait()


def stats_kernel(n, reducers, smoothed, entry, masked, flags, stats, smoothed_out):
    rows, width = smoothed.shape
    segs, blocks = flags.shape
    seg_len = rows // segs
    sensors = masked.shape[1]
    tm, core = lax.axis_index("tm"), lax.axis_index("sens")
    x = smoothed[...]
    ids = row_ids((rows, width))
    weight = jnp.where((tm == n - 1) & (ids == rows - 1), 0.0, 1.0)
    prior = x * weight
    above = pltpu.roll(x, rows - 1, 0)
    above = jnp.where(ids == rows - 1, jnp.broadcast_to(entry[:1], (rows, width)), above)
    size = sensors // blocks
    cross = mm_tn(masked[...], x)
    smoothed_out[...] = x
    lag = jnp.concatenate([mm_tn(prior, x), mm_tn(above, prior)], axis=0)
    held = []
    for g in range(blocks):
        column = jnp.broadcast_to(flags[:, g:g + 1], (segs, width))
        step = jnp.broadcast_to(column[:, None, :], (segs, seg_len, width)).reshape(rows, width)
        held += [mm_tn(x * step, x), cross[g * size:(g + 1) * size]]
    sensor = jnp.concatenate(held, axis=0)
    lag_piece, piece = lag.shape[0] // reducers, sensor.shape[0] // reducers
    for r in range(reducers):
        at = r * (lag_piece + piece)
        stats[at:at + lag_piece] = lag[r * lag_piece:(r + 1) * lag_piece]
        stats[at + lag_piece:at + lag_piece + piece] = sensor[r * piece:(r + 1) * piece]


def sum_kernel(n, reducers, blocks, stats, lag, system, parts, total,
               send, recv, send2, recv2, send3, recv3):
    me, core = lax.axis_index("tm"), lax.axis_index("sens")
    step = n // reducers
    mine, reduces = me // step, me % step == 0
    lag_piece, piece = lag.shape[0] // reducers, system.shape[0] * blocks // reducers
    per_system = reducers // blocks
    groups = n // blocks
    both = lag_piece + piece
    barrier = pltpu.get_barrier_semaphore()

    def peer(k):
        return lax.rem(me + k, n)

    def greet(k, carry):
        pl.semaphore_signal(barrier, inc=1, device_id=(peer(k), core), device_id_type=MESH)
        return carry

    lax.fori_loop(1, n, greet, 0)
    pl.semaphore_wait(barrier, n - 1)

    def part_of(c):
        return stats.at[pl.ds(pl.multiple_of(c * both, both), both)]

    def give(k):
        c = lax.rem(mine + k, reducers)
        return remote(part_of(c), parts.at[me], send.at[k], recv.at[me], (c * step, core))

    def scatter(k, carry):
        give(k).start()
        return carry

    def sent(k, carry):
        give(k).wait_send()
        return carry

    def land(k, carry):
        c = peer(k)
        remote(part_of(0), parts.at[c], send.at[0], recv.at[c], (c, core)).wait_recv()
        return carry

    lax.fori_loop(1, reducers, scatter, 0)
    if step > 1:
        @pl.when(me % step != 0)
        def _():
            give(0).start()

    task, slot = mine // per_system, mine % per_system
    lag_at = pl.ds(pl.multiple_of(mine * lag_piece, lag_piece), lag_piece)
    system_at = pl.ds(pl.multiple_of(slot * piece, piece), piece)
    lag_part, system_part = total.at[pl.ds(0, lag_piece)], total.at[pl.ds(lag_piece, piece)]

    def tell(k):
        return remote(lag_part, lag.at[lag_at], send2.at[k], recv2.at[mine], (peer(k), core))

    def place(g):
        return lax.rem(me // blocks + g, groups) * blocks + task

    def hand(g):
        return remote(system_part, system.at[system_at], send3.at[g], recv3.at[slot], (place(g), core))

    @pl.when(reduces)
    def _():
        lax.fori_loop(1, n, land, 0)
        parts[me] = part_of(mine)[...]
        total[...] = jnp.sum(parts[...], axis=0)
        lag[lag_at] = total[:lag_piece]

        def spread(g, carry):
            @pl.when(place(g) != me)
            def _():
                hand(g).start()
            return carry

        lax.fori_loop(0, groups, spread, 0)

        @pl.when(me % blocks == task)
        def _():
            system[system_at] = total[lag_piece:]

        def announce(k, carry):
            tell(k).start()
            return carry

        lax.fori_loop(1, n, announce, 0)

    def take(j, carry):
        @pl.when((me % blocks * per_system + j) * step != me)
        def _():
            remote(system_part, system.at[pl.ds(pl.multiple_of(j * piece, piece), piece)],
                   send3.at[0], recv3.at[j], (peer(1), core)).wait_recv()
        return carry

    lax.fori_loop(0, per_system, take, 0)

    def hear(r, carry):
        @pl.when(r * step != me)
        def _():
            remote(lag_part, lag.at[pl.ds(pl.multiple_of(r * lag_piece, lag_piece), lag_piece)],
                   send2.at[0], recv2.at[r], (peer(1), core)).wait_recv()
        return carry

    lax.fori_loop(0, reducers, hear, 0)
    lax.fori_loop(1, reducers, sent, 0)
    if step > 1:
        @pl.when(me % step != 0)
        def _():
            give(0).wait_send()

    @pl.when(reduces)
    def _():
        def told(k, carry):
            tell(k).wait_send()
            return carry

        def handed(g, carry):
            @pl.when(place(g) != me)
            def _():
                hand(g).wait_send()
            return carry

        lax.fori_loop(1, n, told, 0)
        lax.fori_loop(0, groups, handed, 0)


def share_kernel(blocks, solved, new_sensing, send, recv):
    me, core = lax.axis_index("tm"), lax.axis_index("sens")
    size = solved.shape[0]
    task = lax.rem(me, blocks)
    base = me - task
    barrier = pltpu.get_barrier_semaphore()
    peers = [(base + lax.rem(task + k, blocks), core) for k in range(1, blocks)]
    for peer in peers:
        pl.semaphore_signal(barrier, inc=1, device_id=peer, device_id_type=MESH)
    pl.semaphore_wait(barrier, blocks - 1)

    def at(t):
        return pl.ds(pl.multiple_of(t * size, size), size)

    for k, peer in enumerate(peers):
        remote(solved, new_sensing.at[at(task)], send.at[k], recv.at[k], peer).start()
    new_sensing[at(task)] = solved[...]
    for k, peer in enumerate(peers):
        source = lax.rem(task - k - 1 + blocks, blocks)
        remote(solved, new_sensing.at[at(source)], send.at[k], recv.at[k], peer).wait()


def inverse_factor(a):
    count, size = a.shape[:2]
    shape = (count, size, 2 * size)
    wide = (count, 1, 2 * size)
    rows = lax.broadcasted_iota(jnp.int32, shape, 1)
    cols = lax.broadcasted_iota(jnp.int32, shape, 2)
    a = jnp.concatenate([a, jnp.where(rows + size == cols, 1.0, 0.0)[:, :, size:]], axis=2)
    scale = jnp.zeros(shape, F32)
    for k in range(0, size, TOGETHER):
        own = range(TOGETHER)
        pivot = [[jnp.broadcast_to(a[:, k + i:k + i + 1, k + j:k + j + 1], wide) if j >= i else None
                  for j in own] for i in own]
        r = [a[:, k + i:k + i + 1, :] for i in own]
        c = [jnp.broadcast_to(a[:, :, k + i:k + i + 1], shape) for i in own]
        for i in own:
            inv = 1.0 / pivot[i][i]
            scale = jnp.where(rows == k + i, inv, scale)
            for j in range(i + 1, TOGETHER):
                m = pivot[i][j] * inv
                for l in range(j, TOGETHER):
                    pivot[j][l] = pivot[j][l] - m * pivot[i][l]
                r[j] = r[j] - m * r[i]
                c[j] = c[j] - m * c[i]
            a = a - jnp.where(rows > k + i, c[i] * inv, 0.0) * r[i]
    return (a * jnp.sqrt(scale))[:, :, size:]


def solve_kernel(ridge, lag, system, new_transition, solved):
    width = lag.shape[1]
    size = solved.shape[0]
    eye = jnp.where(
        row_ids((width, width)) == lax.broadcasted_iota(jnp.int32, (width, width), 1), ridge, 0.0)
    left = system[width:].T
    left = jnp.concatenate([left] * (width // size), axis=1)
    rest = [jnp.concatenate([lag[:width] + eye, lag[width:].T], axis=1),
            jnp.concatenate([system[:width] + eye, left], axis=1)]
    both = range(2)
    steps = width // PIVOT
    inverses, panels = [], []
    for j in range(steps):
        lo, hi = j * PIVOT, (j + 1) * PIVOT
        inv = inverse_factor(jnp.stack([rest[s][:PIVOT, lo:hi] for s in both]))
        panel = [mm(inv[s], rest[s][:PIVOT]) for s in both]
        inverses.append(inv)
        panels.append(panel)
        if hi < width:
            rest = [rest[s][PIVOT:] - mm_tn(panel[s][:, :width], panel[s])[hi:] for s in both]
    x = [None, None]
    for j in reversed(range(steps)):
        hi = (j + 1) * PIVOT
        for s in both:
            rhs = panels[j][s][:, width:]
            if x[s] is not None:
                full = jnp.concatenate([jnp.zeros((hi, width), F32), x[s]], axis=0)
                rhs = rhs - mm(panels[j][s][:, :width], full)
            piece = mm_tn(inverses[j][s], rhs)
            x[s] = piece if x[s] is None else jnp.concatenate([piece, x[s]], axis=0)
    new_transition[...] = x[0].T
    solved[...] = x[1].T[:size]


def on_device(n, telemetry, present, transition, sensing, filter_gain, smooth_gain, initial_state):
    width = transition.shape[0]
    rows, sensors = telemetry.shape
    segs, blocks = present.shape
    seg_len = rows // segs
    half, half_segs = rows // 2, segs // 2
    dma = pltpu.SemaphoreType.DMA
    flags = present.astype(F32)
    wide_flags = jnp.pad(flags, ((0, 0), (0, 128 - blocks)))
    start = jnp.broadcast_to(initial_state[None], (8, width))

    masked, push, corr = vmem_call(
        push_kernel,
        (shaped(rows, sensors), shaped(rows, width), shaped(blocks, width, width)),
        in_specs=in_vmem(5),
    )(telemetry, flags, transition, sensing, filter_gain)
    push_in, corr_in, flags_in = vmem_call(
        pair_kernel,
        (shaped(half, width), shaped(blocks, width, width), shaped(segs, 128)),
        [dma((3,)), dma((3,))],
        in_vmem(3), remote=1,
    )(push, corr, wide_flags)
    levels = seg_len.bit_length() - 1
    scalars = pl.BlockSpec(memory_space=pltpu.SMEM)
    powers, ends, local, chunk = vmem_call(
        functools.partial(maps_kernel, seg_len),
        (shaped(levels, half_segs, width, width), shaped(half_segs, width, width),
         shaped(half, width), shaped(width + 8, width)),
        [VMEM((half_segs, width + 8, width), F32)],
        in_vmem(4) + [scalars, scalars] + in_vmem(1),
    )(push, push_in, corr, corr_in, wide_flags, flags_in, transition)
    entry = vmem_call(
        functools.partial(carry_kernel, n),
        shaped(8, width),
        [VMEM((width + 8, width), F32), VMEM((width + 8, width), F32),
         VMEM((GROUP - 1, width + 8, width), F32), VMEM((8, width), F32), VMEM((8, width), F32),
         dma((GROUP + 1,)), dma((GROUP + 1,))],
        in_vmem(2), remote=2,
    )(chunk, start)
    back_levels = half.bit_length() - 1
    drive_scan, gains, shift, final = vmem_call(
        functools.partial(filter_kernel, n, seg_len),
        (shaped(half, width), shaped(back_levels + 1, width, width), shaped(8, width),
         shaped(8, width)),
        [VMEM((half_segs, 8, width), F32), VMEM((half, width), F32)],
        in_vmem(6),
    )(entry, powers, ends, local, transition, smooth_gain)
    smoothed, entry_back = vmem_call(
        functools.partial(smooth_kernel, n),
        (shaped(rows, width), shaped(8, width)),
        [VMEM((2 * n, 8, width), F32), dma((2 * n,)), dma((2 * n + 1,))],
        in_vmem(4), remote=3,
    )(drive_scan, gains, shift, final)
    size = sensors // blocks
    reducers = min(n, REDUCERS)
    high = 2 * width + blocks * (width + size)
    stats, smoothed = vmem_call(
        functools.partial(stats_kernel, n, reducers),
        (shaped(high, width), shaped(rows, width)),
        in_specs=in_vmem(4),
    )(smoothed, entry_back, masked, flags)
    lag, system = vmem_call(
        functools.partial(sum_kernel, n, reducers, blocks),
        (shaped(2 * width, width), shaped(width + size, width)),
        [VMEM((n, high // reducers, width), F32), VMEM((high // reducers, width), F32),
         dma((reducers,)), dma((n,)), dma((n,)), dma((reducers,)),
         dma((n // blocks,)), dma((reducers // blocks,))],
        in_vmem(1), remote=4,
    )(stats)
    new_transition, solved = vmem_call(
        functools.partial(solve_kernel, RIDGE * rows * n),
        (shaped(width, width), shaped(size, width)),
        in_specs=in_vmem(2),
    )(lag, system)
    new_sensing = vmem_call(
        functools.partial(share_kernel, blocks),
        shaped(sensors, width),
        [dma((blocks - 1,)), dma((blocks - 1,))],
        in_vmem(1), remote=5,
    )(solved)
    return (new_transition, new_sensing, smoothed)


def solution(mesh):
    placed = (P("tm", "sens"), P("tm", "sens"), P(), P("sens", None), P(None, "sens"), P(), P())
    return jax.shard_map(
        functools.partial(on_device, mesh.shape["tm"]),
        mesh=mesh,
        in_specs=placed,
        out_specs=(P(), P("sens", None), P("tm", None)),
        check_vma=False,
    )
```

profile of v0, /device:TPU:0, one launch (start us, length us, event | category | flops | bytes accessed | tf_op | source)
XLA Modules:
  0.0 122.0 jit_solution(13201467910990862167)
XLA Ops:
  0.6 0.8 copy.10
  1.4 0.0 copy-start
  1.4 0.8 copy-done
  2.2 0.0 copy-start.3
  2.2 1.0 copy-done.3
  3.3 0.9 copy-done.4
  4.2 0.9 copy-done.5
  5.1 2.1 %shard_map.94 = (f32[512,256]{1,0:T(8,128)S(1)}, f32[512,128]{1,0:T(8,128)S(1)}, f32[4,128,128]{2,1,0:T(8,128)S(1)}) custom-call(f32[512,256]{1,0:T(8,128)S(1)} %copy-done.3, f32[32,4]{1,0:T(8,128)S(1)} %convert_element_type.5.flags, f32[128,128]{1,0:T(8,128)S(1)} %copy-done, f32[256,128]{1,0:T(8,128)S(1)} %copy-done.4, f32[128,256]{1,0:T(8,128)S(1)} %copy-done.5), custom_call_target="tpu_custom_call" | custom-call | tf_op jit(solution)/shard_map/pallas_call | solution.py:595
  7.2 1.9 %shard_map.95 = (f32[256,128]{1,0:T(8,128)S(1)}, f32[4,128,128]{2,1,0:T(8,128)S(1)}, f32[32,128]{1,0:T(8,128)S(1)}) custom-call(f32[512,128]{1,0:T(8,128)S(1)} %get-tuple-element.25.push, f32[4,128,128]{2,1,0:T(8,128)S(1)} %get-tuple-element.26.corr, f32[32,128]{1,0:T(8,128)S(1)} %pad.4.flags), custom_call_target="tpu_custom_call" | custom-call | tf_op jit(solution)/shard_map/pallas_call | solution.py:600
  9.1 0.0 copy-start.1
  9.1 0.8 copy-done.1
  9.9 14.3 %shard_map.96 = (f32[4,16,128,128]{3,2,1,0:T(8,128)}, f32[16,128,128]{2,1,0:T(8,128)S(1)}, f32[256,128]{1,0:T(8,128)S(1)}, f32[136,128]{1,0:T(8,128)S(1)}) custom-call(f32[512,128]{1,0:T(8,128)S(1)} %get-tuple-element.25.push, f32[256,128]{1,0:T(8,128)S(1)} %get-tuple-element.27.push_in, f32[4,128,128]{2,1,0:T(8,128)S(1)} %get-tuple-element.26.corr, ...), custom_call_target="tpu_custom_call" | custom-call | tf_op jit(solution)/shard_map/pallas_call | solution.py:608
  24.3 0.7 broadcast_in_dim.2.start
  24.9 14.5 %shard_map.97.entry = f32[8,128]{1,0:T(8,128)S(1)} custom-call(f32[136,128]{1,0:T(8,128)S(1)} %get-tuple-element.30.chunk, f32[8,128]{1,0:T(8,128)S(1)} %broadcast_in_dim.2.start), custom_call_target="tpu_custom_call" | custom-call | tf_op jit(solution)/shard_map/pallas_call | solution.py:615
  39.5 0.0 copy-start.2
  39.5 0.8 copy-done.2
  40.3 0.8 copy-done.6
  41.1 17.3 %shard_map.98 = (f32[256,128]{1,0:T(8,128)S(1)}, f32[9,128,128]{2,1,0:T(8,128)S(1)}, f32[8,128]{1,0:T(8,128)S(1)}, f32[8,128]{1,0:T(8,128)S(1)}) custom-call(f32[8,128]{1,0:T(8,128)S(1)} %shard_map.97.entry, f32[4,16,128,128]{3,2,1,0:T(8,128)} %get-tuple-element.31.powers, f32[16,128,128]{2,1,0:T(8,128)S(1)} %get-tuple-element.32.ends, ...), custom_call_target="tpu_custom_call" | custom-call | tf_op jit(solution)/shard_map/pallas_call | solution.py:624
  58.4 18.7 %shard_map.99 = (f32[512,128]{1,0:T(8,128)S(1)}, f32[8,128]{1,0:T(8,128)S(1)}) custom-call(f32[256,128]{1,0:T(8,128)S(1)} %get-tuple-element.34.drive_scan, f32[9,128,128]{2,1,0:T(8,128)S(1)} %get-tuple-element.35.gains, f32[8,128]{1,0:T(8,128)S(1)} %get-tuple-element.36.shift, f32[8,128]{1,0:T(8,128)S(1)} %get-tuple-element.37.final), custom_call_target="tpu_custom_call" | custom-call | tf_op jit(solution)/shard_map/pallas_call | solution.py:631
  77.1 1.9 %shard_map.100 = (f32[1024,128]{1,0:T(8,128)S(1)}, f32[512,128]{1,0:T(8,128)}) custom-call(f32[512,128]{1,0:T(8,128)S(1)} %get-tuple-element.38.smoothed, f32[8,128]{1,0:T(8,128)S(1)} %get-tuple-element.39.entry, f32[512,256]{1,0:T(8,128)S(1)} %get-tuple-element.40.masked, f32[32,4]{1,0:T(8,128)S(1)} %convert_element_type.5.flags), custom_call_target="tpu_custom_call" | custom-call | tf_op jit(solution)/shard_map/pallas_call | solution.py:640
  79.0 28.2 %shard_map.101 = (f32[256,128]{1,0:T(8,128)S(1)}, f32[192,128]{1,0:T(8,128)S(1)}) custom-call(f32[1024,128]{1,0:T(8,128)S(1)} %get-tuple-element.41.stats), custom_call_target="tpu_custom_call" | custom-call | tf_op jit(solution)/shard_map/pallas_call | solution.py:645
  107.2 9.2 %shard_map.102 = (f32[128,128]{1,0:T(8,128)}, f32[64,128]{1,0:T(8,128)S(1)}) custom-call(f32[256,128]{1,0:T(8,128)S(1)} %get-tuple-element.42.lag, f32[192,128]{1,0:T(8,128)S(1)} %get-tuple-element.43.system), custom_call_target="tpu_custom_call" | custom-call | tf_op jit(solution)/shard_map/pallas_call | solution.py:653
  116.5 4.9 %shard_map.103 = f32[256,128]{1,0:T(8,128)S(1)} custom-call(f32[64,128]{1,0:T(8,128)S(1)} %get-tuple-element.45.solved), custom_call_target="tpu_custom_call" | custom-call | tf_op jit(solution)/shard_map/pallas_call | solution.py:658
  121.3 0.7 copy.12
  (5 shorter events, 0.0 us)
Async XLA Ops:
  1.4 0.8 copy-start
  2.2 1.0 copy-start.3
  3.3 0.9 copy-start.4
  4.2 0.9 copy-start.5
  9.1 0.8 copy-start.1
  39.5 0.8 copy-start.2
  40.3 0.8 copy-start.6
where the time goes:
time: 122 us
  Pallas kernels  113 us (93%)
  local copies, waits for them, and re-layouts  8.28 us (7%)
    pallas_call x1, Pallas kernels, on_device(): vmem_call(functools.partial(sum_kernel, n, reducers, blocks), (shaped(2 *...  28.2 us
    pallas_call x1, Pallas kernels, on_device(): vmem_call(functools.partial(smooth_kernel, n), (shaped(rows, width), shap...  18.7 us
    pallas_call x1, Pallas kernels, on_device(): vmem_call(functools.partial(filter_kernel, n, seg_len), (shaped(half, wid...  17.3 us
    pallas_call x1, Pallas kernels, on_device(): vmem_call(functools.partial(carry_kernel, n), shaped(8, width), [VMEM((wi...  14.5 us
    pallas_call x1, Pallas kernels, on_device(): vmem_call(functools.partial(maps_kernel, seg_len), (shaped(levels, half_s...  14.3 us
    pallas_call x1, Pallas kernels, on_device(): vmem_call(functools.partial(solve_kernel, RIDGE * rows * n), (shaped(widt...  9.24 us
    unnamed x16, local copies, waits for them, and re-layouts  7.62 us
    pallas_call x1, Pallas kernels, on_device(): vmem_call(functools.partial(share_kernel, blocks), shaped(sensors, width)...  4.87 us

commit v1 on v0

--- a/solution.py
+++ b/solution.py
@@ -18,7 +18,23 @@
 LIMIT = 48 * 1024 * 1024
 
 
+def terms(x):
+    one = x.astype(jnp.bfloat16)
+    rest = x - one.astype(F32)
+    two = rest.astype(jnp.bfloat16)
+    return one, two, (rest - two.astype(F32)).astype(jnp.bfloat16)
+
+
 def mm(a, b):
+    if a.shape[0] % 16 == 0 and a.shape[1] == b.shape[1] == 128:
+        a1, a2, a3 = terms(a)
+        b1, b2, b3 = terms(b)
+        pair = jnp.concatenate([b1, b2], axis=1)
+        t = jnp.dot(jnp.concatenate([a1, a2], axis=1), jnp.concatenate([pair, pair], axis=0),
+                    preferred_element_type=F32)
+        u = jnp.dot(jnp.concatenate([a1, a3], axis=1), jnp.concatenate([b3, b1], axis=0),
+                    preferred_element_type=F32)
+        return t[:, :128] + (t[:, 128:] + u)
     return jnp.dot(a, b, precision=lax.Precision.HIGHEST, preferred_element_type=F32)
 
 
@@ -79,14 +95,24 @@
     return jax.ShapeDtypeStruct(shape, F32)
 
 
-def push_kernel(tele, flags, trans, sense, gain, masked, push, corr):
+def push_kernel(tele, present, trans, sense, gain, smooth, start,
+                masked, push, corr, flags, trans_out, smooth_out, start_out):
     rows, sensors = tele.shape
-    segs, blocks = flags.shape
+    blocks, segs = present.shape
     seg_len, width = rows // segs, sensors // blocks
-    spread = jnp.where(
-        lax.broadcasted_iota(jnp.int32, (blocks, sensors), 1) // width
-        == lax.broadcasted_iota(jnp.int32, (blocks, sensors), 0), 1.0, 0.0)
-    wide = jnp.dot(flags[...], spread, preferred_element_type=F32)
+    trans_out[...] = trans[...]
+    smooth_out[...] = smooth[...]
+    start_out[...] = jnp.broadcast_to(start[...], start_out.shape)
+
+    def placed(columns, each):
+        spread = jnp.where(
+            lax.broadcasted_iota(jnp.int32, (blocks, columns), 1) // each
+            == lax.broadcasted_iota(jnp.int32, (blocks, columns), 0), 1.0, 0.0)
+        return lax.dot_general(present[...].astype(F32), spread, (((0,), (0,)), ((), ())),
+                               preferred_element_type=F32)
+
+    flags[...] = placed(128, 1)
+    wide = placed(sensors, width)
     step = jnp.broadcast_to(wide[:, None, :], (segs, seg_len, sensors)).reshape(rows, sensors)
     values = tele[...] * step
     masked[...] = values
@@ -344,9 +370,9 @@
     swap.wait()
 
 
-def stats_kernel(n, reducers, smoothed, entry, masked, flags, stats, smoothed_out):
+def stats_kernel(n, blocks, reducers, smoothed, entry, masked, flags, stats, smoothed_out):
     rows, width = smoothed.shape
-    segs, blocks = flags.shape
+    segs = flags.shape[0]
     seg_len = rows // segs
     sensors = masked.shape[1]
     tm, core = lax.axis_index("tm"), lax.axis_index("sens")
@@ -588,21 +614,18 @@
     seg_len = rows // segs
     half, half_segs = rows // 2, segs // 2
     dma = pltpu.SemaphoreType.DMA
-    flags = present.astype(F32)
-    wide_flags = jnp.pad(flags, ((0, 0), (0, 128 - blocks)))
-    start = jnp.broadcast_to(initial_state[None], (8, width))
-
-    masked, push, corr = vmem_call(
+    masked, push, corr, flags, transition, smooth_gain, start = vmem_call(
         push_kernel,
-        (shaped(rows, sensors), shaped(rows, width), shaped(blocks, width, width)),
-        in_specs=in_vmem(5),
-    )(telemetry, flags, transition, sensing, filter_gain)
+        (shaped(rows, sensors), shaped(rows, width), shaped(blocks, width, width),
+         shaped(segs, 128), shaped(width, width), shaped(width, width), shaped(8, width)),
+        in_specs=in_vmem(7),
+    )(telemetry, present.T, transition, sensing, filter_gain, smooth_gain, initial_state[None])
     push_in, corr_in, flags_in = vmem_call(
         pair_kernel,
         (shaped(half, width), shaped(blocks, width, width), shaped(segs, 128)),
         [dma((3,)), dma((3,))],
         in_vmem(3), remote=1,
-    )(push, corr, wide_flags)
+    )(push, corr, flags)
     levels = seg_len.bit_length() - 1
     scalars = pl.BlockSpec(memory_space=pltpu.SMEM)
     powers, ends, local, chunk = vmem_call(
@@ -611,7 +634,7 @@
          shaped(half, width), shaped(width + 8, width)),
         [VMEM((half_segs, width + 8, width), F32)],
         in_vmem(4) + [scalars, scalars] + in_vmem(1),
-    )(push, push_in, corr, corr_in, wide_flags, flags_in, transition)
+    )(push, push_in, corr, corr_in, flags, flags_in, transition)
     entry = vmem_call(
         functools.partial(carry_kernel, n),
         shaped(8, width),
@@ -638,7 +661,7 @@
     reducers = min(n, REDUCERS)
     high = 2 * width + blocks * (width + size)
     stats, smoothed = vmem_call(
-        functools.partial(stats_kernel, n, reducers),
+        functools.partial(stats_kernel, n, blocks, reducers),
         (shaped(high, width), shaped(rows, width)),
         in_specs=in_vmem(4),
     )(smoothed, entry_back, masked, flags)

time: 122 us -> 117 us (0.959)
  Pallas kernels: 113 us -> 110 us
  local copies, waits for them, and re-layouts: 8.28 us -> 6.51 us
    pallas_call x1, Pallas kernels: 17.3 us -> 15.7 us  [on_device(): vmem_call(functools.partial(filter_kernel, n, seg_len), (shaped(half, wid...]
    unnamed x16 -> x15, local copies, waits for them, and re-layouts: 7.62 us -> 6.51 us
where the time goes in v1:
time: 117 us
  Pallas kernels  110 us (94%)
  local copies, waits for them, and re-layouts  6.51 us (6%)
    pallas_call x1, Pallas kernels, on_device(): vmem_call(functools.partial(sum_kernel, n, reducers, blocks), (shaped(2 *...  28.3 us
    pallas_call x1, Pallas kernels, on_device(): vmem_call(functools.partial(smooth_kernel, n), (shaped(rows, width), shap...  18.4 us
    pallas_call x1, Pallas kernels, on_device(): vmem_call(functools.partial(filter_kernel, n, seg_len), (shaped(half, wid...  15.7 us
    pallas_call x1, Pallas kernels, on_device(): vmem_call(functools.partial(carry_kernel, n), shaped(8, width), [VMEM((wi...  14.4 us
    pallas_call x1, Pallas kernels, on_device(): vmem_call(functools.partial(maps_kernel, seg_len), (shaped(levels, half_s...  13.6 us
    pallas_call x1, Pallas kernels, on_device(): vmem_call(functools.partial(solve_kernel, RIDGE * rows * n), (shaped(widt...  8.45 us
    unnamed x15, local copies, waits for them, and re-layouts  6.51 us
    pallas_call x1, Pallas kernels, on_device(): vmem_call(functools.partial(share_kernel, blocks), shaped(sensors, width)...  4.87 us

profile of v1, /device:TPU:0, one launch (start us, length us, event | category | flops | bytes accessed | tf_op | source)
XLA Modules:
  0.0 116.8 jit_solution(10391431840255437075)
XLA Ops:
  0.6 0.0 copy-start
  0.6 1.0 copy-done
  1.7 0.0 copy-start.1
  1.7 0.9 copy-done.1
  2.6 0.0 copy-start.2
  2.6 0.9 copy-done.2
  3.5 0.0 copy-start.3
  3.5 0.8 copy-done.3
  4.3 0.0 copy-start.4
  4.3 0.8 copy-done.4
  5.2 0.0 copy-start.5
  5.2 0.7 copy-done.5
  5.8 0.7 copy-done.6
  6.5 2.1 %shard_map.94 = (f32[512,256]{1,0:T(8,128)S(1)}, f32[512,128]{1,0:T(8,128)S(1)}, f32[4,128,128]{2,1,0:T(8,128)S(1)}, f32[32,128]{1,0:T(8,128)S(1)}, f32[128,128]...) custom-call(f32[512,256]{1,0:T(8,128)S(1)} %copy-done, s32[4,32]{1,0:T(4,128)S(1)} %bitcast.2, ...), custom_call_target="tpu_custom_call" | custom-call | tf_op jit(solution)/shard_map/pallas_call | solution.py:617
  8.6 1.9 %shard_map.95 = (f32[256,128]{1,0:T(8,128)S(1)}, f32[4,128,128]{2,1,0:T(8,128)S(1)}, f32[32,128]{1,0:T(8,128)S(1)}) custom-call(f32[512,128]{1,0:T(8,128)S(1)} %get-tuple-element.29.push, f32[4,128,128]{2,1,0:T(8,128)S(1)} %get-tuple-element.30.corr, f32[32,128]{1,0:T(8,128)S(1)} %get-tuple-element.31.flags), custom_call_target="tpu_custom_call" | custom-call | tf_op jit(solution)/shard_map/pallas_call | solution.py:623
  10.6 13.6 %shard_map.96 = (f32[4,16,128,128]{3,2,1,0:T(8,128)}, f32[16,128,128]{2,1,0:T(8,128)S(1)}, f32[256,128]{1,0:T(8,128)S(1)}, f32[136,128]{1,0:T(8,128)S(1)}) custom-call(f32[512,128]{1,0:T(8,128)S(1)} %get-tuple-element.29.push, f32[256,128]{1,0:T(8,128)S(1)} %get-tuple-element.32.push_in, f32[4,128,128]{2,1,0:T(8,128)S(1)} %get-tuple-element.30.corr, ...), custom_call_target="tpu_custom_call" | custom-call | tf_op jit(solution)/shard_map/pallas_call | solution.py:631
  24.1 14.4 %shard_map.97.entry = f32[8,128]{1,0:T(8,128)S(1)} custom-call(f32[136,128]{1,0:T(8,128)S(1)} %get-tuple-element.36.chunk, f32[8,128]{1,0:T(8,128)S(1)} %get-tuple-element.37.start), custom_call_target="tpu_custom_call" | custom-call | tf_op jit(solution)/shard_map/pallas_call | solution.py:638
  38.5 15.7 %shard_map.98 = (f32[256,128]{1,0:T(8,128)S(1)}, f32[9,128,128]{2,1,0:T(8,128)S(1)}, f32[8,128]{1,0:T(8,128)S(1)}, f32[8,128]{1,0:T(8,128)S(1)}) custom-call(f32[8,128]{1,0:T(8,128)S(1)} %shard_map.97.entry, f32[4,16,128,128]{3,2,1,0:T(8,128)} %get-tuple-element.38.powers, f32[16,128,128]{2,1,0:T(8,128)S(1)} %get-tuple-element.39.ends, ...), custom_call_target="tpu_custom_call" | custom-call | tf_op jit(solution)/shard_map/pallas_call | solution.py:647
  54.2 18.4 %shard_map.99 = (f32[512,128]{1,0:T(8,128)S(1)}, f32[8,128]{1,0:T(8,128)S(1)}) custom-call(f32[256,128]{1,0:T(8,128)S(1)} %get-tuple-element.42.drive_scan, f32[9,128,128]{2,1,0:T(8,128)S(1)} %get-tuple-element.43.gains, f32[8,128]{1,0:T(8,128)S(1)} %get-tuple-element.44.shift, f32[8,128]{1,0:T(8,128)S(1)} %get-tuple-element.45.final), custom_call_target="tpu_custom_call" | custom-call | tf_op jit(solution)/shard_map/pallas_call | solution.py:654
  72.6 1.9 %shard_map.100 = (f32[1024,128]{1,0:T(8,128)S(1)}, f32[512,128]{1,0:T(8,128)}) custom-call(f32[512,128]{1,0:T(8,128)S(1)} %get-tuple-element.46.smoothed, f32[8,128]{1,0:T(8,128)S(1)} %get-tuple-element.47.entry, f32[512,256]{1,0:T(8,128)S(1)} %get-tuple-element.48.masked, f32[32,128]{1,0:T(8,128)S(1)} %get-tuple-element.31.flags), custom_call_target="tpu_custom_call" | custom-call | tf_op jit(solution)/shard_map/pallas_call | solution.py:663
  74.5 28.3 %shard_map.101 = (f32[256,128]{1,0:T(8,128)S(1)}, f32[192,128]{1,0:T(8,128)S(1)}) custom-call(f32[1024,128]{1,0:T(8,128)S(1)} %get-tuple-element.49.stats), custom_call_target="tpu_custom_call" | custom-call | tf_op jit(solution)/shard_map/pallas_call | solution.py:668
  102.8 8.4 %shard_map.102 = (f32[128,128]{1,0:T(8,128)}, f32[64,128]{1,0:T(8,128)S(1)}) custom-call(f32[256,128]{1,0:T(8,128)S(1)} %get-tuple-element.50.lag, f32[192,128]{1,0:T(8,128)S(1)} %get-tuple-element.51.system), custom_call_target="tpu_custom_call" | custom-call | tf_op jit(solution)/shard_map/pallas_call | solution.py:676
  111.2 4.9 %shard_map.103 = f32[256,128]{1,0:T(8,128)S(1)} custom-call(f32[64,128]{1,0:T(8,128)S(1)} %get-tuple-element.53.solved), custom_call_target="tpu_custom_call" | custom-call | tf_op jit(solution)/shard_map/pallas_call | solution.py:681
  116.1 0.7 copy.11
  (1 shorter events, 0.0 us)
Async XLA Ops:
  0.6 1.0 copy-start
  1.7 0.9 copy-start.1
  2.6 0.9 copy-start.2
  3.5 0.8 copy-start.3
  4.3 0.8 copy-start.4
  5.2 0.7 copy-start.5
  5.8 0.7 copy-start.6
